TPU v7x, 32 devices: a whole 2x2x4 slice. The times are simulated.
32 devices in a mesh: groups: 2 (over y), seq: 4 (over z), head: 2 (over x), rep: 2 (over core).
Axes of the slice: x: 2, y: 2, z: 4, core: 2. Of those that a mesh axis runs over, the one named last changes fastest.
Arguments:
- queries: bfloat16 [8192, 2048], P(('groups', 'seq'), ('head', 'rep')), parts along dimension 0, may hold values from -8 to 8
- keys_values: bfloat16 [2, 8192, 2048], P(None, ('groups', 'seq'), ('head', 'rep')), parts along dimension 1, may hold values from -8 to 8
- pack_pos: int32 [1024], P('groups'), parts along dimension 0, may hold values from 0 to 4095
- bounds: int32 [2, 8192], P(None, ('groups', 'seq')), parts along dimension 1, may hold values from 0 to 4096, as said below
- radius: int32 [32], P(('head', 'rep')), may hold values from 128 to 512, as said below
- pack_proj: bfloat16 [2, 2048, 2048], P(None, None, ('head', 'rep')), may hold values from -0.5 to 0.5
Outputs:
- mixed: bfloat16 [8192, 2048], P(('groups', 'seq'), ('head', 'rep')), parts along dimension 0
There are 2 independent parts, one for each index of `groups`. A program takes and returns all parts, laid end to end along the dimension named above; an argument that names none is the same for every part. Nothing has to cross between parts.
Inputs may be any that keep to these rules, and one draw needn't show every extreme that they name: bounds[0, s] and bounds[1, s] are the first position and the end (exclusive) of the document of token s; the 8 documents are contiguous and tile the sequence. Some head has radius exactly 512.
All inputs are finite; a program needn't handle non-finite values.
Results may differ from a plain program's by a relative error of at most 0.012.
Values may be sent and summed in bfloat16 or wider, within the bound.
A program may use at most 128 MiB of HBM per device.

v0:
```python
import math
import jax
import jax.numpy as jnp
from jax import lax
from jax.sharding import PartitionSpec as P

HEAD_DIM = 64
PACK = 512
RADIUS = 512


def padded(cells, sides, width):
    for axis, dim in sides:
        count = lax.axis_size(axis)
        ends = count - 1
        head = lax.slice_in_dim(cells, 0, width, axis=dim)
        tail = lax.slice_in_dim(cells, cells.shape[dim] - width, cells.shape[dim], axis=dim)
        cells = jnp.concatenate(
            [
                lax.ppermute(tail, axis, [(i, (i + 1) % count) for i in range(ends)]),
                cells,
                lax.ppermute(head, axis, [((i + 1) % count, i) for i in range(ends)]),
            ],
            axis=dim,
        )
    return cells


def divide_heads(summed, totals):
    rows_here, heads_here = totals.shape
    shaped = summed.reshape(rows_here, heads_here, -1) / totals[:, :, None]
    return shaped.reshape(rows_here, -1)


def attend(
    query_block,
    window_keys,
    window_values,
    pack_key_heads,
    pack_value_heads,
    lower,
    upper,
    radius,
    first_pos,
):
    rows_here = query_block.shape[0]
    window_len = window_keys.shape[0]
    scale = 1.0 / math.sqrt(HEAD_DIM)
    pack_scores = (
        jnp.einsum("qhd,phd->hqp", query_block, pack_key_heads, preferred_element_type=jnp.float32)
        * scale
    )
    window_scores = (
        jnp.einsum("qhd,khd->hqk", query_block, window_keys, preferred_element_type=jnp.float32)
        * scale
    )
    query_pos = first_pos + jnp.arange(rows_here, dtype=jnp.int32)
    key_pos = first_pos - RADIUS + jnp.arange(window_len, dtype=jnp.int32)
    distance = jnp.abs(key_pos[None, :] - query_pos[:, None])
    inside = (key_pos[None, :] >= lower[:, None]) & (key_pos[None, :] < upper[:, None])
    allowed = (distance[None, :, :] <= radius[:, None, None]) & inside[None, :, :]
    window_scores = jnp.where(allowed, window_scores, -1e30)
    highest = jnp.maximum(jnp.max(pack_scores, axis=2), jnp.max(window_scores, axis=2))
    pack_weights = jnp.exp(pack_scores - highest[:, :, None])
    window_weights = jnp.exp(window_scores - highest[:, :, None])
    totals = jnp.sum(pack_weights, axis=2) + jnp.sum(window_weights, axis=2)
    summed = jnp.einsum(
        "hqp,phd->qhd",
        pack_weights.astype(jnp.bfloat16),
        pack_value_heads,
        preferred_element_type=jnp.float32,
    )
    summed = summed + jnp.einsum(
        "hqk,khd->qhd",
        window_weights.astype(jnp.bfloat16),
        window_values,
        preferred_element_type=jnp.float32,
    )
    return (summed / totals.T[:, :, None]).reshape(rows_here, -1).astype(jnp.bfloat16)


def shards(queries, keys_values, pack_pos, bounds, radius, pack_proj):
    tokens_here, width = queries.shape
    heads_here = radius.shape[0]
    scale = 1.0 / math.sqrt(HEAD_DIM)
    offset_pos = lax.axis_index("seq") * tokens_here
    local_pos = pack_pos - offset_pos
    selector = (local_pos[:, None] == jnp.arange(tokens_here, dtype=jnp.int32)[None, :]).astype(
        jnp.bfloat16
    )
    picked = jnp.dot(selector, queries, preferred_element_type=jnp.float32)
    picked_share = lax.psum_scatter(
        picked.astype(jnp.bfloat16), "seq", scatter_dimension=0, tiled=True
    )
    pack_query = lax.all_gather(picked_share, "seq", axis=0, tiled=True)
    query_heads = pack_query.reshape(PACK, heads_here, HEAD_DIM)
    key_heads = keys_values[0].reshape(tokens_here, heads_here, HEAD_DIM)
    value_heads = keys_values[1].reshape(tokens_here, heads_here, HEAD_DIM)
    pack_scores = (
        jnp.einsum("phd,thd->pht", query_heads, key_heads, preferred_element_type=jnp.float32)
        * scale
    )
    local_top = jnp.max(pack_scores, axis=2)
    global_top = lax.pmax(local_top, "seq")
    pack_weights = jnp.exp(pack_scores - global_top[:, :, None])
    row_total = jnp.sum(pack_weights, axis=2)
    row_sum = jnp.einsum(
        "pht,thd->phd",
        pack_weights.astype(jnp.bfloat16),
        value_heads,
        preferred_element_type=jnp.float32,
    ).reshape(PACK, width)
    whole_sum, whole_total = lax.psum((row_sum, row_total), "seq")
    packed = divide_heads(whole_sum, whole_total).astype(jnp.bfloat16)
    portion = lax.all_gather(packed, ("head", "rep"), axis=1, tiled=True)
    key_part = jnp.dot(portion, pack_proj[0], preferred_element_type=jnp.float32)
    value_part = jnp.dot(portion, pack_proj[1], preferred_element_type=jnp.float32)
    pack_keys = key_part.astype(jnp.bfloat16)
    pack_values = value_part.astype(jnp.bfloat16)
    extended = padded(keys_values, (("seq", 1),), RADIUS)
    rows_per = math.gcd(tokens_here, 512)
    window_len = rows_per + 2 * RADIUS
    pack_key_heads = pack_keys.reshape(PACK, heads_here, HEAD_DIM)
    pack_value_heads = pack_values.reshape(PACK, heads_here, HEAD_DIM)

    def token_block(which_block):
        offset_row = which_block * rows_per
        query_block = lax.dynamic_slice_in_dim(queries, offset_row, rows_per, 0).reshape(
            rows_per, heads_here, HEAD_DIM
        )
        window = lax.dynamic_slice_in_dim(extended, offset_row, window_len, 1)
        window_keys = window[0].reshape(window_len, heads_here, HEAD_DIM)
        window_values = window[1].reshape(window_len, heads_here, HEAD_DIM)
        lower = lax.dynamic_slice_in_dim(bounds[0], offset_row, rows_per, 0)
        upper = lax.dynamic_slice_in_dim(bounds[1], offset_row, rows_per, 0)
        return attend(
            query_block,
            window_keys,
            window_values,
            pack_key_heads,
            pack_value_heads,
            lower,
            upper,
            radius,
            offset_pos + offset_row,
        )

    blocks_out = lax.map(token_block, jnp.arange(tokens_here // rows_per, dtype=jnp.int32))
    return blocks_out.reshape(tokens_here, width)


def solution(mesh):
    return jax.shard_map(
        shards,
        mesh=mesh,
        in_specs=(
            P(("groups", "seq"), ("head", "rep")),
            P(None, ("groups", "seq"), ("head", "rep")),
            P("groups"),
            P(None, ("groups", "seq")),
            P(("head", "rep")),
            P(None, None, ("head", "rep")),
        ),
        out_specs=P(("groups", "seq"), ("head", "rep")),
        check_vma=False,
    )
```

profile of v0, /device:TPU:0, one launch (start us, length us, event | category | flops | bytes accessed | tf_op | source)
XLA Modules:
  0.0 283.8 jit_solution(12413389611932709694)
XLA Ops:
  7.2 2.8 fusion.35
  12.8 21.7 %reduce-scatter.2.cloned.1.call-done = bf16[128,512]{1,0:T(8,128)(2,1)} async-done(((bf16[512,512]{1,0:T(8,128)(2,1)}), bf16[128,512]{1,0:T(8,128)(2,1)}) %reduce-scatter.2.cloned.1.call-update) | async-done | bytes 131088 | tf_op jit(solution)/shard_map/reduce_scatter | solution.py:92
  34.5 16.1 %all_gather.6 = bf16[512,512]{1,0:T(8,128)(2,1)S(1)} all-gather(bf16[128,512]{1,0:T(8,128)(2,1)} %reduce-scatter.2.cloned.1.call-done), channel_id=1, replica_groups=mesh['groups'=2,'seq'=4,'head'=2,'rep'=2] {'seq'}, dimensions={0}, use_global_device_ids=true | all-gather | bytes 655360 | tf_op jit(solution)/shard_map/all_gather | solution.py:95
  50.8 8.1 %bitcast_reduce_fusion = (f32[512,8]{0,1:T(8,128)S(1)}, f32[8,512,1024]{2,1,0:T(8,128)}) fusion(bf16[512,8,64]{0,2,1:T(8,128)(2,1)S(1)} %bitcast.103, bf16[1024,8,64]{0,2,1:T(8,128)(2,1)S(1)} %bitcast.102), kind=kOutput, calls=%fused_computation.30 | convolution fusion | flops 545255424 | bytes 18366464 | tf_op jit(solution)/shard_map/phd,thd->pht/dot_general | solution.py:100
  58.9 15.9 %pmax.7 = f32[512,8]{0,1:T(8,128)S(1)} all-reduce(f32[512,8]{0,1:T(8,128)S(1)} %get-tuple-element.185), channel_id=1, replica_groups=mesh['groups'=2,'seq'=4,'head'=2,'rep'=2] {'seq'}, use_global_device_ids=true, to_apply=%region_2.0 | all-reduce | flops 4096 | bytes 32768 | tf_op jit(solution)/shard_map/pmax | solution.py:104
  74.8 8.2 %fusion.26 = f32[8,512,64]{1,2,0:T(8,128)} fusion(bf16[1024,8,64]{0,2,1:T(8,128)(2,1)S(1)} %bitcast.100, f32[8,512,1024]{2,1,0:T(8,128)} %get-tuple-element.186, f32[512,8]{0,1:T(8,128)S(1)} %pmax.7), kind=kOutput, calls=%fused_computation.34 | convolution fusion | flops 549453824 | bytes 18890752 | tf_op jit(solution)/shard_map/pht,thd->phd/dot_general | solution.py:107
  83.0 7.6 %fusion.24 = f32[512,8]{0,1:T(8,128)S(1)} fusion(f32[8,512,1024]{2,1,0:T(8,128)} %get-tuple-element.186, f32[512,8]{0,1:T(8,128)S(1)} %pmax.7), kind=kLoop, calls=%fused_computation.32 | loop fusion | flops 12578816 | bytes 16809984 | tf_op jit(solution)/shard_map/reduce_sum | solution.py:106
  90.7 17.0 %psum.15 = f32[512,8]{0,1:T(8,128)S(1)} all-reduce(f32[512,8]{0,1:T(8,128)S(1)} %fusion.24), channel_id=1, replica_groups=mesh['groups'=2,'seq'=4,'head'=2,'rep'=2] {'seq'}, use_global_device_ids=true, to_apply=%region_5.0 | all-reduce | flops 4096 | bytes 32768 | tf_op jit(solution)/shard_map/psum | solution.py:113
  107.7 25.8 %all-reduce.2.cloned.1.call-done = f32[512,512]{0,1:T(8,128)} async-done(((f32[512,512]{0,1:T(8,128)}), f32[512,512]{0,1:T(8,128)}) %all-reduce.2.cloned.1.call-update) | async-done | bytes 1048592 | tf_op jit(solution)/shard_map/psum | solution.py:113
  135.7 3.0 %copy.20 = bf16[2,1024,512]{1,2,0:T(8,128)(2,1)S(1)} copy(bf16[2,1024,512]{2,1,0:T(8,128)(2,1)} %param.9) | data formatting | bytes 4194304 | tf_op args[1]
  141.2 5.5 %collective-permute-start = (bf16[2,512,512]{1,2,0:T(8,128)(2,1)S(1)}, bf16[2,512,512]{1,2,0:T(8,128)(2,1)}, u32[]{:S(2)}, u32[]{:S(2)}) collective-permute-start(bf16[2,512,512]{1,2,0:T(8,128)(2,1)S(1)} %get-tuple-element.181), channel_id=1, source_target_pairs={{0,4},{4,8},{8,12},{1,5},{5,9},{9,13},{2,6},{6,10},{10,14},{3,7},{... | collective-permute-start | bytes 3145736 | tf_op jit(solution)/shard_map/ppermute | solution.py:20
  146.7 20.5 %collective-permute-done.1 = bf16[2,512,512]{1,2,0:T(8,128)(2,1)} collective-permute-done((bf16[2,512,512]{1,2,0:T(8,128)(2,1)}, bf16[2,512,512]{1,2,0:T(8,128)(2,1)}, u32[]{:S(2)}, u32[]{:S(2)}) %collective-permute-start.1) | collective-permute-done | bytes 1048608 | tf_op jit(solution)/shard_map/ppermute | solution.py:22
  168.1 3.4 %pad_maximum_fusion = bf16[2,2048,512]{1,2,0:T(8,128)(2,1)} fusion(bf16[2,512,512]{1,2,0:T(8,128)(2,1)} %collective-permute-done.1, bf16[2,1024,512]{1,2,0:T(8,128)(2,1)S(1)} %copy.20, bf16[2,512,512]{1,2,0:T(8,128)(2,1)} %collective-permute-done), kind=kLoop, calls=%fused_computation.35 | loop fusion | flops 12582912 | bytes 8388608 | tf_op jit(solution)/shard_map/concatenate | solution.py:18
  171.5 3.5 %fusion.36 = bf16[512,512]{0,1:T(8,128)(2,1)S(1)} fusion(bf16[512,2048]{0,1:T(8,128)(2,1)} %all-gather.2.cloned.1.call-done, bf16[2,2048,512]{2,1,0:T(8,128)(2,1)} %param.13), kind=kOutput, calls=%fused_computation.45 | convolution fusion | flops 1074003968 | bytes 4718592 | tf_op jit(solution)/shard_map/dot_general | solution.py:116
  175.0 4.3 %fusion.39 = bf16[512,512]{0,1:T(8,128)(2,1)} fusion(bf16[512,2048]{0,1:T(8,128)(2,1)} %all-gather.2.cloned.1.call-done, bf16[2,2048,512]{2,1,0:T(8,128)(2,1)} %param.13), kind=kOutput, calls=%fused_computation.46 | convolution fusion | flops 1074003968 | bytes 4718592 | tf_op jit(solution)/shard_map/dot_general | solution.py:117
  179.3 98.0 %while.12 = (s32[]{:T(128)}, bf16[2,512,512]{2,1,0:T(8,128)(2,1)}, s32[2]{0:T(128)S(1)}, bf16[1024,512]{1,0:T(8,128)(2,1)}, bf16[512,8,64]{0,2,1:T(8,128)(2,1)S(...) while((s32[]{:T(128)}, bf16[2,512,512]{2,1,0:T(8,128)(2,1)}, ...), condition=%wide.region_11.12_spmd, body=%wide.region_6.11_spmd.sunk | while | flops 2225596416 | bytes 137660848 | solution.py:148
  180.9 3.3 %constant_dynamic-slice_fusion.8 = (bf16[1,1536,512]{1,2,0:T(8,128)(2,1)}, bf16[1,1536,512]{1,2,0:T(8,128)(2,1)S(1)}) fusion(bf16[2,2048,512]{1,2,0:T(8,128)(2,1)} %get-tuple-element.310, s32[]{:T(128)S(6)} %select_n.24, s32[]{:T(128)S(6)} %add.106), kind=kLoop, calls=%fused_computation.22.clone.1 | loop fusion | bytes 6291464 | tf_op jit(solution)/shard_map/while/body/eval_jaxpr/slice | solution.py:132
  186.7 14.5 %fusion.83 = (f32[8,512]{1,0:T(8,128)S(1)}, f32[8,512,1536]{2,1,0:T(8,128)}) fusion(bf16[512,8,64]{0,2,1:T(8,128)(2,1)S(1)} %bitcast.95, bf16[1536,8,64]{0,2,1:T(8,128)(2,1)} %bitcast.97, pred[512,1536]{1,0:T(8,128)(4,1)S(1)} %compare_and_fusion.2, s32[8]{0:T(128)S(1)} %get-tuple-element.308, s32[512,1536]{1,0:T(8,128)S(1)} %subtract_abs_fusion.2), kind=kOutput, calls=%fused_computation.53.clone.1 | convolution fusion | flops 836759552 | bytes 31211552 | tf_op jit(solution)/shard_map/while/body/eval_jaxpr/qhd,khd->hqk/dot_general | solution.py:54
  202.5 10.3 %fusion.84 = f32[512,8,64]{0,2,1:T(8,128)S(1)} fusion(bf16[1536,8,64]{0,2,1:T(8,128)(2,1)S(1)} %bitcast.94, f32[8,512,1536]{2,1,0:T(8,128)} %get-tuple-element.264, f32[8,512]{1,0:T(8,128)S(1)} %max.13), kind=kOutput, calls=%fused_computation.16.clone.1 | convolution fusion | flops 817889280 | bytes 27803648 | tf_op jit(solution)/shard_map/while/body/eval_jaxpr/hqk,khd->qhd/dot_general | solution.py:73
  214.2 11.3 %fusion.86 = f32[8,512]{1,0:T(8,128)S(1)} fusion(f32[8,512,1536]{2,1,0:T(8,128)} %get-tuple-element.264, f32[8,512]{1,0:T(8,128)S(1)} %max.13), kind=kLoop, calls=%fused_computation.2.clone.1 | loop fusion | flops 12578816 | bytes 25198592 | tf_op jit(solution)/shard_map/while/body/eval_jaxpr/reduce_sum | solution.py:66
  229.8 3.3 %constant_dynamic-slice_fusion.8 = (bf16[1,1536,512]{1,2,0:T(8,128)(2,1)}, bf16[1,1536,512]{1,2,0:T(8,128)(2,1)S(1)}) fusion(bf16[2,2048,512]{1,2,0:T(8,128)(2,1)} %get-tuple-element.310, s32[]{:T(128)S(6)} %select_n.24, s32[]{:T(128)S(6)} %add.106), kind=kLoop, calls=%fused_computation.22.clone.1 | loop fusion | bytes 6291464 | tf_op jit(solution)/shard_map/while/body/eval_jaxpr/slice | solution.py:132
  235.6 14.5 %fusion.83 = (f32[8,512]{1,0:T(8,128)S(1)}, f32[8,512,1536]{2,1,0:T(8,128)}) fusion(bf16[512,8,64]{0,2,1:T(8,128)(2,1)S(1)} %bitcast.95, bf16[1536,8,64]{0,2,1:T(8,128)(2,1)} %bitcast.97, pred[512,1536]{1,0:T(8,128)(4,1)S(1)} %compare_and_fusion.2, s32[8]{0:T(128)S(1)} %get-tuple-element.308, s32[512,1536]{1,0:T(8,128)S(1)} %subtract_abs_fusion.2), kind=kOutput, calls=%fused_computation.53.clone.1 | convolution fusion | flops 836759552 | bytes 31211552 | tf_op jit(solution)/shard_map/while/body/eval_jaxpr/qhd,khd->hqk/dot_general | solution.py:54
  251.4 10.3 %fusion.84 = f32[512,8,64]{0,2,1:T(8,128)S(1)} fusion(bf16[1536,8,64]{0,2,1:T(8,128)(2,1)S(1)} %bitcast.94, f32[8,512,1536]{2,1,0:T(8,128)} %get-tuple-element.264, f32[8,512]{1,0:T(8,128)S(1)} %max.13), kind=kOutput, calls=%fused_computation.16.clone.1 | convolution fusion | flops 817889280 | bytes 27803648 | tf_op jit(solution)/shard_map/while/body/eval_jaxpr/hqk,khd->qhd/dot_general | solution.py:73
  263.1 11.3 %fusion.86 = f32[8,512]{1,0:T(8,128)S(1)} fusion(f32[8,512,1536]{2,1,0:T(8,128)} %get-tuple-element.264, f32[8,512]{1,0:T(8,128)S(1)} %max.13), kind=kLoop, calls=%fused_computation.2.clone.1 | loop fusion | flops 12578816 | bytes 25198592 | tf_op jit(solution)/shard_map/while/body/eval_jaxpr/reduce_sum | solution.py:66
  (66 shorter events, 26.7 us)
Async XLA Ops:
  6.5 28.0 %reduce-scatter.2.cloned.1.call-start = ((), (), s32[]{:S(2)}) async-start(), calls=%async_computation.1 | async-start | bytes 655360 | tf_op jit(solution)/shard_map/reduce_scatter | solution.py:92
  10.0 123.5 %all-reduce.2.cloned.1.call-start = ((), (), s32[]{:S(2)}) async-start(), calls=%async_computation.2 | async-start | bytes 2097152 | tf_op jit(solution)/shard_map/psum | solution.py:113
  83.0 88.5 %all-gather.2.cloned.1.call-start = ((), (), s32[]{:S(2)}) async-start(), calls=%async_computation.3 | async-start | bytes 2621440 | tf_op jit(solution)/shard_map/all_gather | solution.py:115
  139.9 27.3 %collective-permute-start.1 = (bf16[2,512,512]{1,2,0:T(8,128)(2,1)}, bf16[2,512,512]{1,2,0:T(8,128)(2,1)}, u32[]{:S(2)}, u32[]{:S(2)}) collective-permute-start(bf16[2,512,512]{1,2,0:T(8,128)(2,1)} %get-tuple-element.182), channel_id=1, source_target_pairs={{4,0},{8,4},{12,8},{5,1},{9,5},{13,9},{6,2},{10,6},{14,10},{7,3},{... | collective-permute-start | bytes 3145736 | tf_op jit(solution)/shard_map/ppermute | solution.py:22
  141.2 26.9 %collective-permute-start = (bf16[2,512,512]{1,2,0:T(8,128)(2,1)S(1)}, bf16[2,512,512]{1,2,0:T(8,128)(2,1)}, u32[]{:S(2)}, u32[]{:S(2)}) collective-permute-start(bf16[2,512,512]{1,2,0:T(8,128)(2,1)S(1)} %get-tuple-element.181), channel_id=1, source_target_pairs={{0,4},{4,8},{8,12},{1,5},{5,9},{9,13},{2,6},{6,10},{10,14},{3,7},{... | collective-permute-start | bytes 3145736 | tf_op jit(solution)/shard_map/ppermute | solution.py:20
  171.5 7.9 %copy-start = (s32[2,1024]{1,0:T(2,128)S(1)}, s32[2,1024]{1,0:T(2,128)}, u32[]{:S(2)}) copy-start(s32[2,1024]{1,0:T(2,128)} %param.11) | copy-start | bytes 24580
  171.5 7.9 %copy-start.3 = (s32[8]{0:T(128)S(1)}, s32[8]{0:T(128)}, u32[]{:S(2)}) copy-start(s32[8]{0:T(128)} %param.12) | copy-start | bytes 100
  214.2 11.4 %copy-start.4 = (bf16[512,8,64]{0,2,1:T(8,128)(2,1)S(1)}, bf16[512,8,64]{0,2,1:T(8,128)(2,1)}, u32[]{:S(2)}) copy-start(bf16[512,8,64]{0,2,1:T(8,128)(2,1)} %get-tuple-element.311) | copy-start | bytes 1572868 | tf_op jit(solution)/shard_map/while
  225.5 1.9 copy-start.1
  227.5 1.0 copy-start.2
  263.1 11.4 %copy-start.4 = (bf16[512,8,64]{0,2,1:T(8,128)(2,1)S(1)}, bf16[512,8,64]{0,2,1:T(8,128)(2,1)}, u32[]{:S(2)}) copy-start(bf16[512,8,64]{0,2,1:T(8,128)(2,1)} %get-tuple-element.311) | copy-start | bytes 1572868 | tf_op jit(solution)/shard_map/while
  274.4 1.9 copy-start.1
  276.3 1.0 copy-start.2
Sparse Core Ops, SparseCore 0:
  10.1 24.3 reduce-scatter.1
  83.1 50.3 all-reduce.1
  135.8 21.9 all-gather.1
where the time goes:
time: 285 us; the launch traced here: 284 us
  matrix products  82.2 us (29%)
  waiting for transfers between devices  68.9 us (24%)
  blocking collectives  49 us (17%)
  other arithmetic  41.6 us (15%)
  local copies, waits for them, and re-layouts  20.1 us (7%)
  between operations  13.2 us (5%)
  starting transfers between devices  6.9 us (2%)
    dot_general x2, matrix products, attend(): jnp.einsum('qhd,khd->hqk', query_block, window_keys, preferred_element_ty...  28.9 us
    psum x1, waiting for transfers between devices, shards(): whole_sum, whole_total = lax.psum((row_sum, row_total), 'seq')  25.8 us
    reduce_sum x4, other arithmetic, attend(): totals = jnp.sum(pack_weights, axis=2) + jnp.sum(window_weights, axis=2)  25.4 us
    reduce_scatter x1, waiting for transfers between devices, shards(): lax.psum_scatter(picked.astype(jnp.bfloat16), 'seq', scatter_dimension=0,...  21.7 us
    dot_general x2, matrix products, attend(): jnp.einsum('hqk,khd->qhd', window_weights.astype(jnp.bfloat16), window_va...  20.6 us
    ppermute x1, waiting for transfers between devices, padded(): lax.ppermute(head, axis, [((i + 1) % count, i) for i in range(ends)])  20.5 us
    psum x1, blocking collectives, shards(): whole_sum, whole_total = lax.psum((row_sum, row_total), 'seq')  17 us
    all_gather x1, blocking collectives, shards(): pack_query = lax.all_gather(picked_share, 'seq', axis=0, tiled=True)  16.1 us
  transfers between devices with their start and end apart: 5, of which 4 were waited for; matrix products, arithmetic and copies ran while one was open for 6% of the time, Pallas kernels for 0%

commit v1 on v0

--- a/solution.py
+++ b/solution.py
@@ -92,7 +92,15 @@
     picked_share = lax.psum_scatter(
         picked.astype(jnp.bfloat16), "seq", scatter_dimension=0, tiled=True
     )
-    pack_query = lax.all_gather(picked_share, "seq", axis=0, tiled=True)
+    num = lax.axis_size("seq")
+    vals = [(jj, (jj + 1) % num) for jj in range(num)]
+    latest = [None] * num
+    latest[num - 1] = picked_share
+    for kk in range(num - 2, -1, -1):
+        latest[kk] = lax.ppermute(latest[kk + 1], "seq", vals)
+    part_next = jnp.concatenate(latest, 0)
+    tmp = (lax.axis_index("seq") + 1) * picked_share.shape[0]
+    pack_query = jnp.roll(part_next, tmp, 0)
     query_heads = pack_query.reshape(PACK, heads_here, HEAD_DIM)
     key_heads = keys_values[0].reshape(tokens_here, heads_here, HEAD_DIM)
     value_heads = keys_values[1].reshape(tokens_here, heads_here, HEAD_DIM)

time: 285 us -> 291 us (1.021)
  waiting for transfers between devices: 68.9 us -> 89.4 us
  blocking collectives: 49 us -> 32.9 us
    ppermute x0 -> x3, waiting for transfers between devices: none -> 17.8 us  [shards(): latest[kk] = lax.ppermute(latest[kk + 1], 'seq', vals)]
    all_gather x1 -> x0, blocking collectives: 16.1 us -> none  [shards(): pack_query = lax.all_gather(picked_share, 'seq', axis=0, tiled=True)]
  transfers between devices with their start and end apart: 5 -> 8, of which waited for: 4 -> 7; matrix products, arithmetic and copies ran while one was open for 6% -> 6% of each run, Pallas kernels for 0% -> 0%
where the time goes in v1:
time: 291 us; the launch traced here: 290 us
  waiting for transfers between devices  89.4 us (31%)
  matrix products  82.2 us (28%)
  other arithmetic  41.7 us (14%)
  blocking collectives  32.9 us (11%)
  local copies, waits for them, and re-layouts  22.1 us (8%)
  between operations  13.3 us (5%)
  starting transfers between devices  6.91 us (2%)
    dot_general x2, matrix products, attend(): jnp.einsum('qhd,khd->hqk', query_block, window_keys, preferred_element_ty...  28.9 us
    psum x1, waiting for transfers between devices, shards(): whole_sum, whole_total = lax.psum((row_sum, row_total), 'seq')  25.7 us
    reduce_sum x4, other arithmetic, attend(): totals = jnp.sum(pack_weights, axis=2) + jnp.sum(window_weights, axis=2)  25.4 us
    reduce_scatter x1, waiting for transfers between devices, shards(): lax.psum_scatter(picked.astype(jnp.bfloat16), 'seq', scatter_dimension=0,...  24.4 us
    dot_general x2, matrix products, attend(): jnp.einsum('hqk,khd->qhd', window_weights.astype(jnp.bfloat16), window_va...  20.6 us
    ppermute x1, waiting for transfers between devices, padded(): lax.ppermute(head, axis, [((i + 1) % count, i) for i in range(ends)])  20.5 us
    ppermute x3, waiting for transfers between devices, shards(): latest[kk] = lax.ppermute(latest[kk + 1], 'seq', vals)  17.8 us
    psum x1, blocking collectives, shards(): whole_sum, whole_total = lax.psum((row_sum, row_total), 'seq')  17.3 us
  transfers between devices with their start and end apart: 8, of which 7 were waited for; matrix products, arithmetic and copies ran while one was open for 6% of the time, Pallas kernels for 0%

profile of v1, /device:TPU:0, one launch (start us, length us, event | category | flops | bytes accessed | tf_op | source)
XLA Modules:
  0.0 290.4 jit_solution(16665431352732465218)
XLA Ops:
  10.1 24.4 %reduce-scatter.2.cloned.1.call-done = bf16[128,512]{1,0:T(8,128)(2,1)} async-done(((bf16[512,512]{1,0:T(8,128)(2,1)}), bf16[128,512]{1,0:T(8,128)(2,1)}) %reduce-scatter.2.cloned.1.call-update) | async-done | bytes 131088 | tf_op jit(solution)/shard_map/reduce_scatter | solution.py:92
  34.5 7.0 %collective-permute-done = bf16[128,512]{1,0:T(8,128)(2,1)S(1)} collective-permute-done((bf16[128,512]{1,0:T(8,128)(2,1)}, bf16[128,512]{1,0:T(8,128)(2,1)S(1)}, u32[]{:S(2)}, u32[]{:S(2)}) %collective-permute-start) | collective-permute-done | bytes 131104 | tf_op jit(solution)/shard_map/ppermute | solution.py:100
  41.5 6.8 %collective-permute-done.1 = bf16[128,512]{1,0:T(8,128)(2,1)S(1)} collective-permute-done((bf16[128,512]{1,0:T(8,128)(2,1)S(1)}, bf16[128,512]{1,0:T(8,128)(2,1)S(1)}, u32[]{:S(2)}, u32[]{:S(2)}) %collective-permute-start.1) | collective-permute-done | bytes 131104 | tf_op jit(solution)/shard_map/ppermute | solution.py:100
  51.1 4.1 %collective-permute-done.2 = bf16[128,512]{1,0:T(8,128)(2,1)} collective-permute-done((bf16[128,512]{1,0:T(8,128)(2,1)S(1)}, bf16[128,512]{1,0:T(8,128)(2,1)}, u32[]{:S(2)}, u32[]{:S(2)}) %collective-permute-start.2) | collective-permute-done | bytes 131104 | tf_op jit(solution)/shard_map/ppermute | solution.py:100
  57.4 8.1 %bitcast_reduce_fusion = (f32[512,8]{0,1:T(8,128)S(1)}, f32[8,512,1024]{2,1,0:T(8,128)}) fusion(bf16[512,8,64]{0,2,1:T(8,128)(2,1)S(1)} %bitcast.103, bf16[1024,8,64]{0,2,1:T(8,128)(2,1)S(1)} %bitcast.101), kind=kOutput, calls=%fused_computation.30 | convolution fusion | flops 545255424 | bytes 18366464 | tf_op jit(solution)/shard_map/phd,thd->pht/dot_general | solution.py:108
  65.5 15.5 %pmax.7 = f32[512,8]{0,1:T(8,128)S(1)} all-reduce(f32[512,8]{0,1:T(8,128)S(1)} %get-tuple-element.185), channel_id=1, replica_groups=mesh['groups'=2,'seq'=4,'head'=2,'rep'=2] {'seq'}, use_global_device_ids=true, to_apply=%region_2.3 | all-reduce | flops 4096 | bytes 32768 | tf_op jit(solution)/shard_map/pmax | solution.py:112
  81.0 8.2 %fusion.26 = f32[8,512,64]{1,2,0:T(8,128)} fusion(bf16[1024,8,64]{0,2,1:T(8,128)(2,1)S(1)} %bitcast.100, f32[8,512,1024]{2,1,0:T(8,128)} %get-tuple-element.186, f32[512,8]{0,1:T(8,128)S(1)} %pmax.7), kind=kOutput, calls=%fused_computation.34 | convolution fusion | flops 549453824 | bytes 18890752 | tf_op jit(solution)/shard_map/pht,thd->phd/dot_general | solution.py:115
  89.2 7.7 %fusion.24 = f32[512,8]{0,1:T(8,128)S(1)} fusion(f32[8,512,1024]{2,1,0:T(8,128)} %get-tuple-element.186, f32[512,8]{0,1:T(8,128)S(1)} %pmax.7), kind=kLoop, calls=%fused_computation.32 | loop fusion | flops 12578816 | bytes 16809984 | tf_op jit(solution)/shard_map/reduce_sum | solution.py:114
  97.0 17.3 %psum.15 = f32[512,8]{0,1:T(8,128)S(1)} all-reduce(f32[512,8]{0,1:T(8,128)S(1)} %fusion.24), channel_id=1, replica_groups=mesh['groups'=2,'seq'=4,'head'=2,'rep'=2] {'seq'}, use_global_device_ids=true, to_apply=%region_5.6 | all-reduce | flops 4096 | bytes 32768 | tf_op jit(solution)/shard_map/psum | solution.py:121
  114.3 25.7 %all-reduce.2.cloned.1.call-done = f32[512,512]{0,1:T(8,128)} async-done(((f32[512,512]{0,1:T(8,128)}), f32[512,512]{0,1:T(8,128)}) %all-reduce.2.cloned.1.call-update) | async-done | bytes 1048592 | tf_op jit(solution)/shard_map/psum | solution.py:121
  147.7 5.5 %collective-permute-start.3 = (bf16[2,512,512]{1,2,0:T(8,128)(2,1)S(1)}, bf16[2,512,512]{1,2,0:T(8,128)(2,1)}, u32[]{:S(2)}, u32[]{:S(2)}) collective-permute-start(bf16[2,512,512]{1,2,0:T(8,128)(2,1)S(1)} %get-tuple-element.181), channel_id=1, source_target_pairs={{0,4},{4,8},{8,12},{1,5},{5,9},{9,13},{2,6},{6,10},{10,14},{3,7},{... | collective-permute-start | bytes 3145736 | tf_op jit(solution)/shard_map/ppermute | solution.py:20
  153.2 20.5 %collective-permute-done.4 = bf16[2,512,512]{1,2,0:T(8,128)(2,1)} collective-permute-done((bf16[2,512,512]{1,2,0:T(8,128)(2,1)}, bf16[2,512,512]{1,2,0:T(8,128)(2,1)}, u32[]{:S(2)}, u32[]{:S(2)}) %collective-permute-start.4) | collective-permute-done | bytes 1048608 | tf_op jit(solution)/shard_map/ppermute | solution.py:22
  174.6 3.4 %pad_maximum_fusion = bf16[2,2048,512]{1,2,0:T(8,128)(2,1)} fusion(bf16[2,512,512]{1,2,0:T(8,128)(2,1)} %collective-permute-done.4, bf16[2,1024,512]{1,2,0:T(8,128)(2,1)S(1)} %copy.19, bf16[2,512,512]{1,2,0:T(8,128)(2,1)} %collective-permute-done.3), kind=kLoop, calls=%fused_computation.35 | loop fusion | flops 12582912 | bytes 8388608 | tf_op jit(solution)/shard_map/concatenate | solution.py:18
  178.0 3.5 %fusion.36 = bf16[512,512]{0,1:T(8,128)(2,1)S(1)} fusion(bf16[512,2048]{0,1:T(8,128)(2,1)} %all-gather.2.cloned.1.call-done, bf16[2,2048,512]{2,1,0:T(8,128)(2,1)} %param.13), kind=kOutput, calls=%fused_computation.45 | convolution fusion | flops 1074003968 | bytes 4718592 | tf_op jit(solution)/shard_map/dot_general | solution.py:124
  181.5 4.3 %fusion.39 = bf16[512,512]{0,1:T(8,128)(2,1)} fusion(bf16[512,2048]{0,1:T(8,128)(2,1)} %all-gather.2.cloned.1.call-done, bf16[2,2048,512]{2,1,0:T(8,128)(2,1)} %param.13), kind=kOutput, calls=%fused_computation.46 | convolution fusion | flops 1074003968 | bytes 4718592 | tf_op jit(solution)/shard_map/dot_general | solution.py:125
  185.9 98.0 %while.12 = (s32[]{:T(128)}, bf16[2,512,512]{2,1,0:T(8,128)(2,1)}, s32[2]{0:T(128)S(1)}, bf16[1024,512]{1,0:T(8,128)(2,1)}, bf16[512,8,64]{0,2,1:T(8,128)(2,1)S(...) while((s32[]{:T(128)}, bf16[2,512,512]{2,1,0:T(8,128)(2,1)}, ...), condition=%wide.region_11.12_spmd, body=%wide.region_6.11_spmd.sunk | while | flops 2225596416 | bytes 137660848 | solution.py:156
  187.4 3.3 %constant_dynamic-slice_fusion.9 = (bf16[1,1536,512]{1,2,0:T(8,128)(2,1)}, bf16[1,1536,512]{1,2,0:T(8,128)(2,1)S(1)}) fusion(bf16[2,2048,512]{1,2,0:T(8,128)(2,1)} %get-tuple-element.310, s32[]{:T(128)S(6)} %select_n.39, s32[]{:T(128)S(6)} %add.122), kind=kLoop, calls=%fused_computation.22.clone.1 | loop fusion | bytes 6291464 | tf_op jit(solution)/shard_map/while/body/eval_jaxpr/slice | solution.py:140
  193.3 14.5 %fusion.83 = (f32[8,512]{1,0:T(8,128)S(1)}, f32[8,512,1536]{2,1,0:T(8,128)}) fusion(bf16[512,8,64]{0,2,1:T(8,128)(2,1)S(1)} %bitcast.95, bf16[1536,8,64]{0,2,1:T(8,128)(2,1)} %bitcast.97, pred[512,1536]{1,0:T(8,128)(4,1)S(1)} %compare_and_fusion.2, s32[8]{0:T(128)S(1)} %get-tuple-element.308, s32[512,1536]{1,0:T(8,128)S(1)} %subtract_abs_fusion.2), kind=kOutput, calls=%fused_computation.62.clone.1 | convolution fusion | flops 836759552 | bytes 31211552 | tf_op jit(solution)/shard_map/while/body/eval_jaxpr/qhd,khd->hqk/dot_general | solution.py:54
  209.0 10.3 %fusion.84 = f32[512,8,64]{0,2,1:T(8,128)S(1)} fusion(bf16[1536,8,64]{0,2,1:T(8,128)(2,1)S(1)} %bitcast.94, f32[8,512,1536]{2,1,0:T(8,128)} %get-tuple-element.264, f32[8,512]{1,0:T(8,128)S(1)} %max.13), kind=kOutput, calls=%fused_computation.16.clone.1 | convolution fusion | flops 817889280 | bytes 27803648 | tf_op jit(solution)/shard_map/while/body/eval_jaxpr/hqk,khd->qhd/dot_general | solution.py:73
  220.7 11.3 %fusion.86 = f32[8,512]{1,0:T(8,128)S(1)} fusion(f32[8,512,1536]{2,1,0:T(8,128)} %get-tuple-element.264, f32[8,512]{1,0:T(8,128)S(1)} %max.13), kind=kLoop, calls=%fused_computation.2.clone.1 | loop fusion | flops 12578816 | bytes 25198592 | tf_op jit(solution)/shard_map/while/body/eval_jaxpr/reduce_sum | solution.py:66
  236.3 3.3 %constant_dynamic-slice_fusion.9 = (bf16[1,1536,512]{1,2,0:T(8,128)(2,1)}, bf16[1,1536,512]{1,2,0:T(8,128)(2,1)S(1)}) fusion(bf16[2,2048,512]{1,2,0:T(8,128)(2,1)} %get-tuple-element.310, s32[]{:T(128)S(6)} %select_n.39, s32[]{:T(128)S(6)} %add.122), kind=kLoop, calls=%fused_computation.22.clone.1 | loop fusion | bytes 6291464 | tf_op jit(solution)/shard_map/while/body/eval_jaxpr/slice | solution.py:140
  242.1 14.5 %fusion.83 = (f32[8,512]{1,0:T(8,128)S(1)}, f32[8,512,1536]{2,1,0:T(8,128)}) fusion(bf16[512,8,64]{0,2,1:T(8,128)(2,1)S(1)} %bitcast.95, bf16[1536,8,64]{0,2,1:T(8,128)(2,1)} %bitcast.97, pred[512,1536]{1,0:T(8,128)(4,1)S(1)} %compare_and_fusion.2, s32[8]{0:T(128)S(1)} %get-tuple-element.308, s32[512,1536]{1,0:T(8,128)S(1)} %subtract_abs_fusion.2), kind=kOutput, calls=%fused_computation.62.clone.1 | convolution fusion | flops 836759552 | bytes 31211552 | tf_op jit(solution)/shard_map/while/body/eval_jaxpr/qhd,khd->hqk/dot_general | solution.py:54
  257.9 10.3 %fusion.84 = f32[512,8,64]{0,2,1:T(8,128)S(1)} fusion(bf16[1536,8,64]{0,2,1:T(8,128)(2,1)S(1)} %bitcast.94, f32[8,512,1536]{2,1,0:T(8,128)} %get-tuple-element.264, f32[8,512]{1,0:T(8,128)S(1)} %max.13), kind=kOutput, calls=%fused_computation.16.clone.1 | convolution fusion | flops 817889280 | bytes 27803648 | tf_op jit(solution)/shard_map/while/body/eval_jaxpr/hqk,khd->qhd/dot_general | solution.py:73
  269.6 11.3 %fusion.86 = f32[8,512]{1,0:T(8,128)S(1)} fusion(f32[8,512,1536]{2,1,0:T(8,128)} %get-tuple-element.264, f32[8,512]{1,0:T(8,128)S(1)} %max.13), kind=kLoop, calls=%fused_computation.2.clone.1 | loop fusion | flops 12578816 | bytes 25198592 | tf_op jit(solution)/shard_map/while/body/eval_jaxpr/reduce_sum | solution.py:66
  (82 shorter events, 34.4 us)
Async XLA Ops:
  6.5 28.0 %reduce-scatter.2.cloned.1.call-start = ((), (), s32[]{:S(2)}) async-start(), calls=%async_computation.1 | async-start | bytes 655360 | tf_op jit(solution)/shard_map/reduce_scatter | solution.py:92
  10.0 130.0 %all-reduce.2.cloned.1.call-start = ((), (), s32[]{:S(2)}) async-start(), calls=%async_computation.2 | async-start | bytes 2097152 | tf_op jit(solution)/shard_map/psum | solution.py:121
  34.5 21.6 %copy-start = (bf16[128,512]{1,0:T(8,128)(2,1)S(1)}, bf16[128,512]{1,0:T(8,128)(2,1)}, u32[]{:S(2)}) copy-start(bf16[128,512]{1,0:T(8,128)(2,1)} %reduce-scatter.2.cloned.1.call-done) | copy-start | bytes 393220
  34.5 7.0 %collective-permute-start = (bf16[128,512]{1,0:T(8,128)(2,1)}, bf16[128,512]{1,0:T(8,128)(2,1)S(1)}, u32[]{:S(2)}, u32[]{:S(2)}) collective-permute-start(bf16[128,512]{1,0:T(8,128)(2,1)} %reduce-scatter.2.cloned.1.call-done), channel_id=1, source_target_pairs={{0,4},{4,8},{8,12},{12,0},{1,5},{5,9},{9,13},{13,1},{2,6},{6,10},{... | collective-permute-start | bytes 393224 | tf_op jit(solution)/shard_map/ppermute | solution.py:100
  41.5 6.8 %collective-permute-start.1 = (bf16[128,512]{1,0:T(8,128)(2,1)S(1)}, bf16[128,512]{1,0:T(8,128)(2,1)S(1)}, u32[]{:S(2)}, u32[]{:S(2)}) collective-permute-start(bf16[128,512]{1,0:T(8,128)(2,1)S(1)} %collective-permute-done), channel_id=1, source_target_pairs={{0,4},{4,8},{8,12},{12,0},{1,5},{5,9},{9,13},{13,1},{2,6},{6,10},{... | collective-permute-start | bytes 393224 | tf_op jit(solution)/shard_map/ppermute | solution.py:100
  48.3 6.9 %collective-permute-start.2 = (bf16[128,512]{1,0:T(8,128)(2,1)S(1)}, bf16[128,512]{1,0:T(8,128)(2,1)}, u32[]{:S(2)}, u32[]{:S(2)}) collective-permute-start(bf16[128,512]{1,0:T(8,128)(2,1)S(1)} %collective-permute-done.1), channel_id=1, source_target_pairs={{0,4},{4,8},{8,12},{12,0},{1,5},{5,9},{9,13},{13,1},{2,6},{6,10},{... | collective-permute-start | bytes 393224 | tf_op jit(solution)/shard_map/ppermute | solution.py:100
  89.2 88.8 %all-gather.2.cloned.1.call-start = ((), (), s32[]{:S(2)}) async-start(), calls=%async_computation.3 | async-start | bytes 2621440 | tf_op jit(solution)/shard_map/all_gather | solution.py:123
  146.4 27.3 %collective-permute-start.4 = (bf16[2,512,512]{1,2,0:T(8,128)(2,1)}, bf16[2,512,512]{1,2,0:T(8,128)(2,1)}, u32[]{:S(2)}, u32[]{:S(2)}) collective-permute-start(bf16[2,512,512]{1,2,0:T(8,128)(2,1)} %get-tuple-element.182), channel_id=1, source_target_pairs={{4,0},{8,4},{12,8},{5,1},{9,5},{13,9},{6,2},{10,6},{14,10},{7,3},{... | collective-permute-start | bytes 3145736 | tf_op jit(solution)/shard_map/ppermute | solution.py:22
  147.7 26.9 %collective-permute-start.3 = (bf16[2,512,512]{1,2,0:T(8,128)(2,1)S(1)}, bf16[2,512,512]{1,2,0:T(8,128)(2,1)}, u32[]{:S(2)}, u32[]{:S(2)}) collective-permute-start(bf16[2,512,512]{1,2,0:T(8,128)(2,1)S(1)} %get-tuple-element.181), channel_id=1, source_target_pairs={{0,4},{4,8},{8,12},{1,5},{5,9},{9,13},{2,6},{6,10},{10,14},{3,7},{... | collective-permute-start | bytes 3145736 | tf_op jit(solution)/shard_map/ppermute | solution.py:20
  178.0 7.9 %copy-start.1 = (s32[2,1024]{1,0:T(2,128)S(1)}, s32[2,1024]{1,0:T(2,128)}, u32[]{:S(2)}) copy-start(s32[2,1024]{1,0:T(2,128)} %param.11) | copy-start | bytes 24580
  178.0 7.9 %copy-start.4 = (s32[8]{0:T(128)S(1)}, s32[8]{0:T(128)}, u32[]{:S(2)}) copy-start(s32[8]{0:T(128)} %param.12) | copy-start | bytes 100
  220.7 11.4 %copy-start.5 = (bf16[512,8,64]{0,2,1:T(8,128)(2,1)S(1)}, bf16[512,8,64]{0,2,1:T(8,128)(2,1)}, u32[]{:S(2)}) copy-start(bf16[512,8,64]{0,2,1:T(8,128)(2,1)} %get-tuple-element.311) | copy-start | bytes 1572868 | tf_op jit(solution)/shard_map/while
  232.0 1.9 copy-start.2
  234.0 1.0 copy-start.3
  269.6 11.4 %copy-start.5 = (bf16[512,8,64]{0,2,1:T(8,128)(2,1)S(1)}, bf16[512,8,64]{0,2,1:T(8,128)(2,1)}, u32[]{:S(2)}) copy-start(bf16[512,8,64]{0,2,1:T(8,128)(2,1)} %get-tuple-element.311) | copy-start | bytes 1572868 | tf_op jit(solution)/shard_map/while
  280.9 1.9 copy-start.2
  282.9 1.0 copy-start.3
Sparse Core Ops, SparseCore 0:
  10.1 24.3 reduce-scatter.1
  89.3 50.7 all-reduce.1
  142.3 21.9 all-gather.1
